TPU v7x, 512 devices: a whole 4x4x16 slice. The times are simulated.
512 devices in a mesh: section: 2 (over x_hi), gy: 16 (over y, x_lo, core), gx: 16 (over z).
Axes of the slice: x: 4 (x_hi: 2, x_lo: 2; x = x_hi * 2 + x_lo), y: 4, z: 16, core: 2. Of those that a mesh axis runs over, the one named last changes fastest.
Arguments:
- images: bfloat16 [2, 512, 1024, 128], P('section', 'gy', 'gx'), may hold values from -6 to 6
- first_kernel: bfloat16 [3, 3, 128, 128], replicated, may hold values from -0.1875 to 0.1875
- projection: bfloat16 [128, 256], replicated, may hold values from -0.5 to 0.5
- second_kernel: bfloat16 [3, 3, 256, 256], replicated, may hold values from -0.125 to 0.125
- cotangent: bfloat16 [2, 256, 512, 256], P('section', 'gy', 'gx'), may hold values from -0.15625 to 0.15625
Outputs:
- features: bfloat16 [2, 256, 512, 256], P('section', 'gy', 'gx')
- grad_first: float32 [3, 3, 128, 128], replicated
- grad_projection: float32 [128, 256], replicated
- grad_second: float32 [3, 3, 256, 256], replicated
All inputs are finite; a program needn't handle non-finite values.
Results may differ from a plain program's by a relative error of at most 0.014.
Values may be sent and summed in bfloat16 or wider, within the bound.
A program may use at most 64 MiB of HBM per device.

v0:
```python
import jax
import jax.numpy as jnp
from jax import lax
from jax.sharding import PartitionSpec as P


def padded_2(array, sides, width):
    for axis, dim in sides:
        size, length = (lax.axis_size(axis), array.shape[dim])
        up = [(i, (i + 1) % size) for i in range(size - 1)]
        down = [(j, i) for i, j in up]
        last = lax.slice_in_dim(array, length - width, length, axis=dim)
        initial = lax.slice_in_dim(array, 0, width, axis=dim)
        before = lax.ppermute(last, axis, up)
        after = lax.ppermute(initial, axis, down)
        array = jnp.concatenate([before, array, after], axis=dim)
    return array


def from_partner(block, axis, bit):
    count = lax.axis_size(axis)
    route = []
    for low in range(count):
        high = low | 1 << bit
        if high != low and high < count:
            route += [(low, high), (high, low)]
    return lax.ppermute(block, axis, route)


def silu_slope(values):
    sigma = jax.nn.sigmoid(values)
    return sigma * (1.0 + values * (1.0 - sigma))


def conv_forward(padded, kernel, row_count, col_count):
    total = jnp.zeros((row_count * col_count, kernel.shape[3]), jnp.float32)
    for row_tap in range(3):
        for col_tap in range(3):
            piece = padded[row_tap : row_tap + row_count, col_tap : col_tap + col_count].reshape(
                row_count * col_count, padded.shape[2]
            )
            total = total + jnp.dot(
                piece, kernel[row_tap, col_tap], preferred_element_type=jnp.float32
            )
    return total


def conv_slopes(padded, slope, row_count, col_count):
    pieces = []
    for row_tap in range(3):
        for col_tap in range(3):
            piece = padded[row_tap : row_tap + row_count, col_tap : col_tap + col_count].reshape(
                row_count * col_count, padded.shape[2]
            )
            pieces.append(jnp.einsum("pc,pd->cd", piece, slope, preferred_element_type=jnp.float32))
    return jnp.stack(pieces).reshape(3, 3, padded.shape[2], slope.shape[1])


def conv_back(padded, kernel, row_count, col_count):
    total = jnp.zeros((row_count * col_count, kernel.shape[2]), jnp.float32)
    for row_tap in range(3):
        for col_tap in range(3):
            piece = padded[
                2 - row_tap : 2 - row_tap + row_count, 2 - col_tap : 2 - col_tap + col_count
            ].reshape(row_count * col_count, padded.shape[2])
            total = total + jnp.einsum(
                "pd,cd->pc", piece, kernel[row_tap, col_tap], preferred_element_type=jnp.float32
            )
    return total


def first_forward(tile, first_kernel):
    row_count, col_count, channels = tile.shape
    padded = padded_2(tile, (("gy", 0), ("gx", 1)), 1)
    before = conv_forward(padded, first_kernel, row_count, col_count)
    hidden = jax.nn.silu(before).astype(jnp.bfloat16).reshape(row_count, col_count, channels)
    pooled = (
        hidden.astype(jnp.float32)
        .reshape(row_count // 2, 2, col_count // 2, 2, channels)
        .sum(axis=(1, 3))
        * 0.25
    ).astype(jnp.bfloat16)
    return (padded, before, pooled)


def project(pooled, projection):
    half_rows, half_cols, channels = pooled.shape
    flat = jnp.dot(
        pooled.reshape(half_rows * half_cols, channels),
        projection,
        preferred_element_type=jnp.float32,
    )
    return flat.astype(jnp.bfloat16).reshape(half_rows, half_cols, projection.shape[1])


def second_pass(middle, second_kernel, upstream):
    half_rows, half_cols, wide = middle.shape
    padded = padded_2(middle, (("gy", 0), ("gx", 1)), 1)
    before = conv_forward(padded, second_kernel, half_rows, half_cols)
    output = jax.nn.silu(before).astype(jnp.bfloat16).reshape(half_rows, half_cols, wide)
    flat_up = upstream.reshape(half_rows * half_cols, wide).astype(jnp.float32)
    slope = (flat_up * silu_slope(before)).astype(jnp.bfloat16)
    kernel_grad = conv_slopes(padded, slope, half_rows, half_cols)
    slope_padded = padded_2(slope.reshape(half_rows, half_cols, wide), (("gy", 0), ("gx", 1)), 1)
    back = conv_back(slope_padded, second_kernel, half_rows, half_cols).astype(jnp.bfloat16)
    return (output, kernel_grad, back.reshape(half_rows, half_cols, wide))


def projection_back(pooled, back, projection):
    half_rows, half_cols, channels = pooled.shape
    flat_pool = pooled.reshape(half_rows * half_cols, channels)
    flat_back = back.reshape(half_rows * half_cols, back.shape[2])
    grad = jnp.einsum("pc,pd->cd", flat_pool, flat_back, preferred_element_type=jnp.float32)
    pooled_slope = jnp.einsum(
        "pd,cd->pc", flat_back, projection, preferred_element_type=jnp.float32
    )
    return (grad, pooled_slope.astype(jnp.bfloat16).reshape(half_rows, half_cols, channels))


def first_back(padded, before, pooled_slope):
    half_rows, half_cols, channels = pooled_slope.shape
    spread = jnp.broadcast_to(
        (pooled_slope.astype(jnp.float32) * 0.25)[:, None, :, None, :],
        (half_rows, 2, half_cols, 2, channels),
    )
    spread = spread.reshape(4 * half_rows * half_cols, channels)
    slope = (spread * silu_slope(before)).astype(jnp.bfloat16)
    return conv_slopes(padded, slope, 2 * half_rows, 2 * half_cols)


def per_device(images, first_kernel, projection, second_kernel, cotangent):
    padded, before, pooled = first_forward(images[0], first_kernel)
    middle = from_partner(project(pooled, projection), "section", 0)
    output, grad_second, back_far = second_pass(middle, second_kernel, cotangent[0])
    back = from_partner(back_far, "section", 0)
    grad_projection, pooled_slope = projection_back(pooled, back, projection)
    grad_first = first_back(padded, before, pooled_slope)
    grad_first, grad_projection, grad_second = lax.psum(
        (grad_first, grad_projection, grad_second), ("section", "gy", "gx")
    )
    return (output[None], grad_first, grad_projection, grad_second)


def solution(mesh):
    placed = (P("section", "gy", "gx", None), P(), P(), P(), P("section", "gy", "gx", None))
    return jax.shard_map(
        per_device,
        mesh=mesh,
        in_specs=placed,
        out_specs=(P("section", "gy", "gx", None), P(), P(), P()),
        check_vma=False,
    )
```

profile of v0, /device:TPU:2, one launch (start us, length us, event | category | flops | bytes accessed | tf_op | source)
XLA Modules:
  0.0 605.1 jit_solution(15916452577856336045)
XLA Ops:
  7.2 0.8 slice_bitcast_fusion.3
  8.0 1.9 collective-permute-start
  10.0 3.6 collective-permute-start.1
  13.6 1.4 collective-permute-done.1
  15.0 0.9 pad_maximum_fusion.15
  15.9 3.8 collective-permute-start.2
  19.8 1.4 collective-permute-start.3
  21.2 1.3 pad_maximum_fusion.1
  22.8 2.7 collective-permute-done.3
  29.0 0.9 convert_reduce_fusion
  30.1 4.1 collective-permute-start.4
  34.3 8.2 %collective-permute-done.4 = bf16[16,32,256]{2,1,0:T(8,128)(2,1)S(1)} collective-permute-done((bf16[16,32,256]{2,1,0:T(8,128)(2,1)S(1)}, bf16[16,32,256]{2,1,0:T(8,128)(2,1)S(1)}, u32[]{:S(2)}, u32[]{:S(2)}) %collective-permute-start.4) | collective-permute-done | bytes 262176 | tf_op jit(solution)/shard_map/ppermute | solution.py:27
  42.5 2.1 collective-permute-start.5
  44.6 3.5 collective-permute-start.6
  48.1 1.4 collective-permute-done.6
  49.6 3.8 collective-permute-start.7
  53.5 1.3 collective-permute-start.8
  55.3 4.9 collective-permute-done.8
  61.9 0.7 copy-done.7
  62.6 1.1 fusion.26
  64.1 3.1 collective-permute-start.9
  67.2 2.5 collective-permute-start.10
  71.4 1.3 collective-permute-start.11
  72.7 6.0 collective-permute-start.12
  79.0 1.1 collective-permute-done.12
  82.7 4.0 collective-permute-start.13
  87.2 7.4 %collective-permute-done.13 = bf16[16,32,256]{2,1,0:T(8,128)(2,1)S(1)} collective-permute-done((bf16[16,32,256]{2,1,0:T(8,128)(2,1)S(1)}, bf16[16,32,256]{2,1,0:T(8,128)(2,1)S(1)}, u32[]{:S(2)}, u32[]{:S(2)}) %collective-permute-start.13) | collective-permute-done | bytes 262176 | tf_op jit(solution)/shard_map/ppermute | solution.py:27
  99.0 0.9 convolution_bitcast_fusion.9
  99.9 492.5 %all-reduce.3.cloned.1.call-done = (f32[3,3,128,128]{3,2,1,0:T(8,128)}, f32[128,256]{1,0:T(8,128)}, f32[3,3,256,256]{3,2,1,0:T(8,128)}) async-done(((f32[3,3,128,128]{3,2,1,0:T(8,128)}, f32[128,256]{1,0:T(8,128)}, f32[3,3,256,256]{3,2,1,0:T(8,128)}), (f32[3,3,128,128]{3,2,1,0:T(8,128)}, f32[128,256]{1,0:T(8,128)}, f32[3,3,256,256]{3,2,1,0:T(8,128)})) %all-reduce.3.cloned.1.call-update) | async-done | bytes 3080208 | tf_op jit(solution)/shard_map/psum | solution.py:138
  592.4 2.0 copy.32
  594.4 0.7 copy.33
  595.0 3.2 copy.34
  (87 shorter events, 15.9 us)
Async XLA Ops:
  7.2 22.7 %copy-start = (bf16[128,256]{1,0:T(8,128)(2,1)S(1)}, bf16[128,256]{1,0:T(8,128)(2,1)}, u32[]{:S(2)}) copy-start(bf16[128,256]{1,0:T(8,128)(2,1)} %param.7) | copy-start | bytes 196612
  7.2 15.3 %copy-start.5 = (bf16[3,3,128,128]{3,2,1,0:T(8,128)(2,1)S(1)}, bf16[3,3,128,128]{3,2,1,0:T(8,128)(2,1)}, u32[]{:S(2)}) copy-start(bf16[3,3,128,128]{3,2,1,0:T(8,128)(2,1)} %param.6) | copy-start | bytes 884740
  7.2 585.2 %all-reduce.3.cloned.1.call-start = ((), (), s32[]{:S(2)}) async-start(), calls=%async_computation | async-start | bytes 6160384 | tf_op jit(solution)/shard_map/psum | solution.py:138
  8.0 5.6 collective-permute-start
  10.0 5.1 collective-permute-start.1
  15.9 6.9 %collective-permute-start.2 = (bf16[34,1,128]{2,1,0:T(2,128)(2,1)S(1)}, bf16[34,1,128]{2,1,0:T(2,128)(2,1)S(1)}, u32[]{:S(2)}, u32[]{:S(2)}) collective-permute-start(bf16[34,1,128]{2,1,0:T(2,128)(2,1)S(1)} %get-tuple-element.15), channel_id=1, source_target_pairs={{0,1},{1,2},{2,3},{3,4},{4,5},{5,6},{6,7},{7,8},{8,9},{9,10},{10,1... | collective-permute-start | bytes 26120 | tf_op jit(solution)/shard_map/ppermute | solution.py:14
  19.8 5.8 copy-start.1
  19.8 5.8 collective-permute-start.3
  29.9 24.9 %copy-start.2 = (bf16[3,3,256,256]{3,2,1,0:T(8,128)(2,1)S(1)}, bf16[3,3,256,256]{3,2,1,0:T(8,128)(2,1)}, u32[]{:S(2)}) copy-start(bf16[3,3,256,256]{3,2,1,0:T(8,128)(2,1)} %param.8) | copy-start | bytes 3538948
  30.1 12.4 %collective-permute-start.4 = (bf16[16,32,256]{2,1,0:T(8,128)(2,1)S(1)}, bf16[16,32,256]{2,1,0:T(8,128)(2,1)S(1)}, u32[]{:S(2)}, u32[]{:S(2)}) collective-permute-start(bf16[16,32,256]{2,1,0:T(8,128)(2,1)S(1)} %bitcast.328), channel_id=1, source_target_pairs={{0,256},{256,0},{1,257},{257,1},{2,258},{258,2},{3,259},{259,3},{4... | collective-permute-start | bytes 786440 | tf_op jit(solution)/shard_map/ppermute | solution.py:27
  42.5 5.6 collective-permute-start.5
  44.6 4.9 collective-permute-start.6
  49.6 5.6 collective-permute-start.7
  53.5 6.7 %collective-permute-start.8 = (bf16[18,1,256]{2,1,0:T(2,128)(2,1)S(1)}, bf16[18,1,256]{2,1,0:T(2,128)(2,1)S(1)}, u32[]{:S(2)}, u32[]{:S(2)}) collective-permute-start(bf16[18,1,256]{2,1,0:T(2,128)(2,1)S(1)} %get-tuple-element.43), channel_id=1, source_target_pairs={{1,0},{2,1},{3,2},{4,3},{5,4},{6,5},{7,6},{8,7},{9,8},{10,9},{11,1... | collective-permute-start | bytes 27656 | tf_op jit(solution)/shard_map/ppermute | solution.py:15
  61.7 1.0 copy-start.7
  64.1 7.3 %collective-permute-start.9 = (bf16[1,32,256]{2,1,0:T(8,128)(2,1)S(1)}, bf16[1,32,256]{2,1,0:T(8,128)(2,1)S(1)}, u32[]{:S(2)}, u32[]{:S(2)}) collective-permute-start(bf16[1,32,256]{2,1,0:T(8,128)(2,1)S(1)} %get-tuple-element.46), channel_id=1, source_target_pairs={{0,16},{16,32},{32,48},{48,64},{64,80},{80,96},{96,112},{112,128},... | collective-permute-start | bytes 49160 | tf_op jit(solution)/shard_map/ppermute | solution.py:14
  67.2 4.2 collective-permute-start.10
  71.4 7.6 %collective-permute-start.11 = (bf16[18,1,256]{2,1,0:T(2,128)(2,1)S(1)}, bf16[18,1,256]{2,1,0:T(2,128)(2,1)S(1)}, u32[]{:S(2)}, u32[]{:S(2)}) collective-permute-start(bf16[18,1,256]{2,1,0:T(2,128)(2,1)S(1)} %get-tuple-element.37), channel_id=1, source_target_pairs={{1,0},{2,1},{3,2},{4,3},{5,4},{6,5},{7,6},{8,7},{9,8},{10,9},{11,1... | collective-permute-start | bytes 27656 | tf_op jit(solution)/shard_map/ppermute | solution.py:15
  72.7 7.4 %collective-permute-start.12 = (bf16[18,1,256]{2,1,0:T(2,128)(2,1)S(1)}, bf16[18,1,256]{2,1,0:T(2,128)(2,1)S(1)}, u32[]{:S(2)}, u32[]{:S(2)}) collective-permute-start(bf16[18,1,256]{2,1,0:T(2,128)(2,1)S(1)} %get-tuple-element.38), channel_id=1, source_target_pairs={{0,1},{1,2},{2,3},{3,4},{4,5},{5,6},{6,7},{7,8},{8,9},{9,10},{10,1... | collective-permute-start | bytes 27656 | tf_op jit(solution)/shard_map/ppermute | solution.py:14
  82.7 12.0 %collective-permute-start.13 = (bf16[16,32,256]{2,1,0:T(8,128)(2,1)S(1)}, bf16[16,32,256]{2,1,0:T(8,128)(2,1)S(1)}, u32[]{:S(2)}, u32[]{:S(2)}) collective-permute-start(bf16[16,32,256]{2,1,0:T(8,128)(2,1)S(1)} %bitcast.329), channel_id=1, source_target_pairs={{0,256},{256,0},{1,257},{257,1},{2,258},{258,2},{3,259},{259,3},{4... | collective-permute-start | bytes 786440 | tf_op jit(solution)/shard_map/ppermute | solution.py:27
  87.2 8.6 %copy-start.3 = (f32[9,256,256]{2,1,0:T(8,128)}, f32[9,256,256]{2,1,0:T(8,128)S(1)}, u32[]{:S(2)}) copy-start(f32[9,256,256]{2,1,0:T(8,128)S(1)} %fusion.6) | copy-start | bytes 7077892
  99.0 0.9 copy-start.4
  592.4 2.0 copy-start.6
Sparse Core Ops, SparseCore 0:
  100.1 492.3 all-reduce.2
where the time goes:
time: 606 us; the launch traced here: 605 us
  waiting for transfers between devices  520 us (86%)
  starting transfers between devices  42.4 us (7%)
  matrix products  14.9 us (2%)
  between operations  14.7 us (2%)
  local copies, waits for them, and re-layouts  8.72 us (1%)
    psum x1, waiting for transfers between devices, per_device(): lax.psum((grad_first, grad_projection, grad_second), ('section', 'gy', 'g...  492 us
    ppermute x6, starting transfers between devices, padded_2(): before = lax.ppermute(last, axis, up)  20.7 us
    ppermute x2, waiting for transfers between devices, from_partner(): return lax.ppermute(block, axis, route)  15.7 us
    ppermute x6, starting transfers between devices, padded_2(): after = lax.ppermute(initial, axis, down)  13.6 us
  transfers between devices with their start and end apart: 15, of which 8 were waited for; matrix products, arithmetic and copies ran while one was open for 1% of the time, Pallas kernels for 0%

commit v1 on v0

--- a/solution.py
+++ b/solution.py
@@ -136,7 +136,7 @@
     grad_projection, pooled_slope = projection_back(pooled, back, projection)
     grad_first = first_back(padded, before, pooled_slope)
     grad_first, grad_projection, grad_second = lax.psum(
-        (grad_first, grad_projection, grad_second), ("section", "gy", "gx")
+        lax.psum((grad_first, grad_projection, grad_second), "section"), ("gy", "gx")
     )
     return (output[None], grad_first, grad_projection, grad_second)
 

time: 606 us -> 2320 us (3.83)
  the two profiles are of different devices: /device:TPU:2 before, /device:TPU:4 now
where the time goes in v1:
time: 2320 us; the launch traced here: 2310 us
  waiting for transfers between devices  2240 us (97%)
  starting transfers between devices  35.8 us (2%)
    psum x1, waiting for transfers between devices, per_device(): lax.psum(lax.psum((grad_first, grad_projection, grad_second), 'section'),...  2090 us
    psum x1, waiting for transfers between devices, per_device(): lax.psum((grad_first, grad_projection, grad_second), 'section')  113 us
  transfers between devices with their start and end apart: 16, of which 10 were waited for; matrix products, arithmetic and copies ran while one was open for 0% of the time, Pallas kernels for 0%

profile of v1, /device:TPU:4, one launch (start us, length us, event | category | flops | bytes accessed | tf_op | source)
XLA Modules:
  0.0 2314.4 jit_solution(2782414319264625042)
XLA Ops:
  7.2 0.8 slice_bitcast_fusion.3
  8.0 1.7 collective-permute-start
  9.8 1.3 collective-permute-start.1
  11.1 2.8 collective-permute-done.1
  13.8 0.9 pad_maximum_fusion.15
  14.7 3.8 collective-permute-start.2
  18.6 1.4 collective-permute-start.3
  20.0 1.3 pad_maximum_fusion.1
  21.6 2.7 collective-permute-done.3
  27.8 0.9 convert_reduce_fusion
  28.9 4.0 collective-permute-start.4
  32.9 8.4 collective-permute-done.4
  41.3 2.0 collective-permute-start.5
  43.4 1.3 collective-permute-start.6
  44.7 3.4 collective-permute-done.6
  48.2 3.8 collective-permute-start.7
  52.0 1.3 collective-permute-start.8
  53.8 4.8 collective-permute-done.8
  61.1 1.1 fusion.26
  62.6 3.2 collective-permute-start.9
  65.8 1.3 collective-permute-start.10
  68.8 0.7 collective-permute-done.10
  69.6 1.3 collective-permute-start.11
  70.9 6.1 collective-permute-start.12
  77.3 1.1 collective-permute-done.12
  81.0 3.1 collective-permute-start.13
  84.7 8.3 collective-permute-done.13
  97.4 0.9 convolution_bitcast_fusion.9
  98.3 112.7 %all-reduce.7.cloned.1.call-done = (f32[3,3,128,128]{3,2,1,0:T(8,128)}, f32[128,256]{1,0:T(8,128)}, f32[3,3,256,256]{3,2,1,0:T(8,128)}) async-done(((f32[3,3,128,128]{3,2,1,0:T(8,128)}, f32[128,256]{1,0:T(8,128)}, f32[3,3,256,256]{3,2,1,0:T(8,128)}), (f32[3,3,128,128]{3,2,1,0:T(8,128)}, f32[128,256]{1,0:T(8,128)}, f32[3,3,256,256]{3,2,1,0:T(8,128)})) %all-reduce.7.cloned.1.call-update) | async-done | bytes 3080208 | tf_op jit(solution)/shard_map/psum | solution.py:139
  211.0 2090.7 %all-reduce.5.cloned.1.call-done = (f32[3,3,128,128]{3,2,1,0:T(8,128)}, f32[128,256]{1,0:T(8,128)}, f32[3,3,256,256]{3,2,1,0:T(8,128)}) async-done(((f32[3,3,128,128]{3,2,1,0:T(8,128)}, f32[128,256]{1,0:T(8,128)}, f32[3,3,256,256]{3,2,1,0:T(8,128)}), (f32[3,3,128,128]{3,2,1,0:T(8,128)}, f32[128,256]{1,0:T(8,128)}, f32[3,3,256,256]{3,2,1,0:T(8,128)})) %all-reduce.5.cloned.1.call-update) | async-done | bytes 3080208 | tf_op jit(solution)/shard_map/psum | solution.py:138
  2301.8 2.0 copy.35
  2304.4 3.2 copy.37
  (90 shorter events, 17.3 us)
Async XLA Ops:
  7.2 21.5 copy-start
  7.2 14.1 copy-start.5
  7.2 203.8 %all-reduce.7.cloned.1.call-start = ((), (), s32[]{:S(2)}) async-start(), calls=%async_computation.1 | async-start | bytes 6160384 | tf_op jit(solution)/shard_map/psum | solution.py:139
  8.0 3.0 collective-permute-start
  9.8 4.1 collective-permute-start.1
  14.7 6.9 collective-permute-start.2
  18.6 5.8 copy-start.1
  18.6 5.8 collective-permute-start.3
  28.6 24.7 %copy-start.2 = (bf16[3,3,256,256]{3,2,1,0:T(8,128)(2,1)S(1)}, bf16[3,3,256,256]{3,2,1,0:T(8,128)(2,1)}, u32[]{:S(2)}) copy-start(bf16[3,3,256,256]{3,2,1,0:T(8,128)(2,1)} %param.8) | copy-start | bytes 3538948
  28.9 12.4 collective-permute-start.4
  41.3 3.3 collective-permute-start.5
  43.4 4.7 collective-permute-start.6
  48.2 5.6 collective-permute-start.7
  52.0 6.6 collective-permute-start.8
  60.2 1.0 copy-start.7
  62.6 6.2 collective-permute-start.9
  65.8 3.7 collective-permute-start.10
  69.6 7.7 collective-permute-start.11
  70.9 7.5 collective-permute-start.12
  81.0 12.0 collective-permute-start.13
  84.7 9.4 copy-start.3
  97.3 0.9 copy-start.4
  98.3 2203.5 %all-reduce.5.cloned.1.call-start = ((), (), s32[]{:S(2)}) async-start(), calls=%async_computation | async-start | bytes 6160384 | tf_op jit(solution)/shard_map/psum | solution.py:138
  2301.8 2.0 copy-start.6
Sparse Core Ops, SparseCore 0:
  98.4 112.5 all-reduce.6
  214.4 2087.2 all-reduce.4
